TPU v7x, 256 devices: a whole 4x4x8 slice. The times are simulated.
256 devices in a mesh: blk: 64 (over y, x_lo, z), row: 4 (over x_hi, core).
Axes of the slice: x: 4 (x_hi: 2, x_lo: 2; x = x_hi * 2 + x_lo), y: 4, z: 8, core: 2. Of those that a mesh axis runs over, the one named last changes fastest.
Arguments:
- matrix: bfloat16 [49152, 16384], P(('row', 'blk'))
- pairing: int32 [2, 64, 4], replicated, may hold values from 0 to 3, each once within a row
Outputs:
- rotated_matrix: bfloat16 [49152, 16384], P(('row', 'blk'))
Inputs may be any that keep to these rules, and one draw needn't show every extreme that they name: pairing[t, g] names each of the 4 slots once.
All inputs are finite; a program needn't handle non-finite values.
Results may differ from a plain program's by a relative error of at most 0.0062.
Values may be sent and summed in bfloat16 or wider, within the bound.
A program may use at most 128 MiB of HBM per device.

v0:
```python
import jax
import jax.numpy as jnp
from jax import lax
from jax.sharding import PartitionSpec as P

BW = 64
BLK_DEV = 4
STEPS = 2


precise = lax.Precision.HIGHEST


def from_behind(block, axis, distance):
    devices = range(lax.axis_size(axis))
    route = [((i - distance) % len(devices), i) for i in devices]
    return lax.ppermute(block, axis, route)


def pair_rotation(cross_raw, squares):
    block_width = cross_raw.shape[0]
    col_scale = 1.0 / jnp.sqrt(squares + 1e-06)
    cross = 0.5 * cross_raw * col_scale[:block_width, None] * col_scale[None, block_width:]
    identity = jnp.eye(block_width, dtype=jnp.float32)
    left_factor = jnp.linalg.cholesky(identity + jnp.dot(cross, cross.T, precision=precise))
    right_factor = jnp.linalg.cholesky(identity + jnp.dot(cross.T, cross, precision=precise))
    left_inverse = jax.scipy.linalg.solve_triangular(left_factor, identity, lower=True).T
    right_inverse = jax.scipy.linalg.solve_triangular(right_factor, identity, lower=True).T
    upper_half = jnp.concatenate(
        [left_inverse, jnp.dot(cross, right_inverse, precision=precise)], axis=1
    )
    lower_half = jnp.concatenate(
        [-jnp.dot(cross.T, left_inverse, precision=precise), right_inverse], axis=1
    )
    return jnp.concatenate([upper_half, lower_half], axis=0).astype(jnp.bfloat16)


def columns_layout(matrix, pairing):
    columns = lax.all_to_all(matrix, "blk", split_axis=1, concat_axis=0, tiled=True)
    couple_count = BLK_DEV // 2
    group_index = lax.axis_index("blk")
    for turn_index in range(STEPS):
        slot_order = lax.dynamic_index_in_dim(pairing[turn_index], group_index, 0, keepdims=False)
        pieces = [
            lax.dynamic_slice_in_dim(columns, slot_order[which] * BW, BW, 1)
            for which in range(BLK_DEV)
        ]
        couples = [
            jnp.concatenate([pieces[2 * which], pieces[2 * which + 1]], axis=1)
            for which in range(couple_count)
        ]
        gram_sums = jnp.stack(
            [jnp.dot(couple.T, couple, preferred_element_type=jnp.float32) for couple in couples]
        )
        gram_sums = lax.psum(gram_sums, "row")
        crosses = gram_sums[:, :BW, BW:]
        squares = jnp.diagonal(gram_sums, axis1=1, axis2=2)
        rotated = [
            jnp.dot(
                couples[which],
                pair_rotation(crosses[which], squares[which]),
                preferred_element_type=jnp.float32,
            ).astype(jnp.bfloat16)
            for which in range(couple_count)
        ]
        staying = [block[:, :BW] for block in rotated]
        moving = jnp.concatenate([block[:, BW:] for block in rotated], axis=1)
        moving = from_behind(moving, "blk", 1)
        layout = []
        for which in range(couple_count):
            layout.append(staying[which])
            layout.append(moving[:, which * BW : (which + 1) * BW])
        columns = jnp.concatenate(layout, axis=1)
    restored = lax.all_to_all(columns, "blk", split_axis=0, concat_axis=1, tiled=True)
    return restored


def local(matrix, pairing):
    return columns_layout(matrix, pairing)


def solution(mesh):
    placed = (P(("row", "blk"), None), P())
    return jax.shard_map(
        local, mesh=mesh, in_specs=placed, out_specs=P(("row", "blk"), None), check_vma=False
    )
```

profile of v0, /device:TPU:1, one launch (start us, length us, event | category | flops | bytes accessed | tf_op | source)
XLA Modules:
  0.0 740.5 jit_solution(16753789492539339298)
XLA Ops:
  6.5 6.3 copy.94
  12.9 13.9 %all-to-all-start = ((bf16[192,64,256]{2,0,1:T(8,128)(2,1)}), bf16[192,64,256]{2,0,1:T(8,128)(2,1)}, u32[]{:S(2)}, u32[]{:S(2)}) async-start(bf16[192,64,256]{2,0,1:T(8,128)(2,1)} %bitcast.171), calls=%async_computation | async-start | bytes 12582912 | tf_op jit(solution)/shard_map/all_to_all | solution.py:39
  30.0 134.8 %all-to-all-done = bf16[192,64,256]{2,0,1:T(8,128)(2,1)} async-done(((bf16[192,64,256]{2,0,1:T(8,128)(2,1)}), bf16[192,64,256]{2,0,1:T(8,128)(2,1)}, u32[]{:S(2)}, u32[]{:S(2)}) %all-to-all-start) | async-done | bytes 6291488 | tf_op jit(solution)/shard_map/all_to_all | solution.py:39
  164.7 6.4 constant_dynamic-slice_fusion.8
  171.2 3.8 convolution_bitcast_fusion.1
  175.0 3.8 convolution_bitcast_fusion
  179.6 45.8 %all-reduce.3.cloned.1.call-done = f32[2,128,128]{2,1,0:T(8,128)} async-done(((f32[2,128,128]{2,1,0:T(8,128)}), f32[2,128,128]{2,1,0:T(8,128)}) %all-reduce.3.cloned.1.call-update) | async-done | bytes 131088 | tf_op jit(solution)/shard_map/psum | solution.py:55
  225.4 17.3 %copy.63 = f32[2,128,128]{0,2,1:T(8,128)} copy(f32[2,128,128]{2,1,0:T(8,128)} %all-reduce.3.cloned.1.call-done) | data formatting | bytes 262144 | tf_op jit(solution)/shard_map/psum | solution.py:55
  242.8 1.8 gather_fusion
  245.2 5.8 cholesky.134
  252.5 4.9 custom-call.16
  258.1 5.8 cholesky.145
  265.4 4.9 custom-call.17
  271.0 4.7 convolution_convert_fusion.3
  275.7 1.9 fusion.147
  278.0 5.8 cholesky.156
  285.2 4.9 custom-call.18
  290.7 5.8 cholesky.167
  297.9 4.9 custom-call.19
  303.5 3.8 convolution_convert_fusion.2
  307.6 1.2 copy-done.4
  308.8 1.9 pad_maximum_fusion.4
  310.7 1.3 collective-permute-start
  315.0 69.8 %collective-permute-done = bf16[12288,128]{0,1:T(8,128)(2,1)} collective-permute-done((bf16[12288,128]{0,1:T(8,128)(2,1)}, bf16[12288,128]{0,1:T(8,128)(2,1)}, u32[]{:S(2)}, u32[]{:S(2)}) %collective-permute-start) | collective-permute-done | bytes 3145760 | tf_op jit(solution)/shard_map/ppermute | solution.py:17
  384.8 2.2 fusion.148
  388.2 1.0 fusion.2
  389.9 1.0 fusion.3
  391.6 42.7 %all-reduce.5.cloned.1.call-done = f32[2,128,128]{2,1,0:T(8,128)} async-done(((f32[2,128,128]{2,1,0:T(8,128)}), f32[2,128,128]{2,1,0:T(8,128)}) %all-reduce.5.cloned.1.call-update) | async-done | bytes 131088 | tf_op jit(solution)/shard_map/psum | solution.py:55
  434.3 5.6 copy.72
  439.9 1.8 gather_fusion.1
  442.3 5.8 cholesky.178
  448.2 0.7 compare_reduce_fusion.3
  449.6 4.9 custom-call.20
  455.1 5.8 cholesky.189
  462.5 4.9 custom-call.21
  468.1 1.1 convolution_convert_fusion.1
  469.8 5.8 cholesky.200
  475.7 0.7 compare_reduce_fusion.1
  477.1 4.9 custom-call.22
  482.6 5.8 cholesky.211
  489.9 4.9 custom-call.23
  495.6 3.0 convolution_convert_fusion
  499.1 1.4 collective-permute-start.1
  500.4 72.5 %collective-permute-done.1 = bf16[12288,128]{0,1:T(8,128)(2,1)S(1)} collective-permute-done((bf16[12288,128]{0,1:T(8,128)(2,1)S(1)}, bf16[12288,128]{0,1:T(8,128)(2,1)S(1)}, u32[]{:S(2)}, u32[]{:S(2)}) %collective-permute-start.1) | collective-permute-done | bytes 3145760 | tf_op jit(solution)/shard_map/ppermute | solution.py:17
  573.2 3.1 pad_maximum_fusion.1
  576.3 8.7 %copy.81 = bf16[12288,256]{1,0:T(8,128)(2,1)} copy(bf16[12288,256]{0,1:T(8,128)(2,1)} %pad_maximum_fusion.1) | data formatting | bytes 12582912 | tf_op jit(solution)/shard_map/concatenate | solution.py:73
  584.9 145.0 %all_to_all.38 = bf16[64,192,256]{2,1,0:T(8,128)(2,1)S(1)} all-to-all(bf16[64,192,256]{2,1,0:T(8,128)(2,1)} %bitcast.172), channel_id=1, replica_groups=mesh['blk'=64,'row'=4] {'blk'}, dimensions={0} | all-to-all | bytes 12582912 | tf_op jit(solution)/shard_map/all_to_all | solution.py:74
  729.9 3.4 copy.92
  (113 shorter events, 22.9 us)
Async XLA Ops:
  12.9 14.0 %copy-start.9 = (s32[2,64,4]{1,2,0:T(4,128)S(1)}, s32[2,64,4]{1,2,0:T(4,128)}, u32[]{:S(2)}) copy-start(s32[2,64,4]{1,2,0:T(4,128)} %param.6) | copy-start | bytes 6148
  12.9 151.9 %all-to-all-start = ((bf16[192,64,256]{2,0,1:T(8,128)(2,1)}), bf16[192,64,256]{2,0,1:T(8,128)(2,1)}, u32[]{:S(2)}, u32[]{:S(2)}) async-start(bf16[192,64,256]{2,0,1:T(8,128)(2,1)} %bitcast.171), calls=%async_computation | async-start | bytes 12582912 | tf_op jit(solution)/shard_map/all_to_all | solution.py:39
  26.8 198.6 %all-reduce.3.cloned.1.call-start = ((), (), s32[]{:S(2)}) async-start(), calls=%async_computation.2 | async-start | bytes 262144 | tf_op jit(solution)/shard_map/psum | solution.py:55
  171.1 3.8 copy-start.1
  171.2 3.8 copy-start
  171.2 7.7 %copy-start.2 = (bf16[12288,64]{1,0:T(8,128)(2,1)}, bf16[12288,64]{1,0:T(8,128)(2,1)S(1)}, u32[]{:S(2)}) copy-start(bf16[12288,64]{1,0:T(8,128)(2,1)S(1)} %get-tuple-element.22) | copy-start | bytes 4718596
  179.5 254.8 %all-reduce.5.cloned.1.call-start = ((), (), s32[]{:S(2)}) async-start(), calls=%async_computation.3 | async-start | bytes 262144 | tf_op jit(solution)/shard_map/psum | solution.py:55
  225.4 19.5 %copy-start.7 = (f32[2,128,128]{2,1,0:T(8,128)S(1)}, f32[2,128,128]{2,1,0:T(8,128)}, u32[]{:S(2)}) copy-start(f32[2,128,128]{2,1,0:T(8,128)} %all-reduce.3.cloned.1.call-done) | copy-start | bytes 393220
  307.3 1.4 copy-start.4
  310.7 74.1 %collective-permute-start = (bf16[12288,128]{0,1:T(8,128)(2,1)}, bf16[12288,128]{0,1:T(8,128)(2,1)}, u32[]{:S(2)}, u32[]{:S(2)}) collective-permute-start(bf16[12288,128]{0,1:T(8,128)(2,1)} %pad_maximum_fusion.4), channel_id=1, source_target_pairs={{252,0},{0,4},{4,8},{8,12},{12,16},{16,20},{20,24},{24,28},{28,32}... | collective-permute-start | bytes 9437192 | tf_op jit(solution)/shard_map/ppermute | solution.py:17
  315.0 72.0 %copy-start.3 = (bf16[12288,64]{0,1:T(8,128)(2,1)S(1)}, bf16[12288,64]{0,1:T(8,128)(2,1)}, u32[]{:S(2)}) copy-start(bf16[12288,64]{0,1:T(8,128)(2,1)} %get-tuple-element.29) | copy-start | bytes 4718596
  388.2 1.1 copy-start.5
  388.2 1.7 copy-start.6
  434.3 7.7 %copy-start.8 = (f32[2,128,128]{2,1,0:T(8,128)S(1)}, f32[2,128,128]{2,1,0:T(8,128)}, u32[]{:S(2)}) copy-start(f32[2,128,128]{2,1,0:T(8,128)} %all-reduce.5.cloned.1.call-done) | copy-start | bytes 393220
  499.1 73.8 %collective-permute-start.1 = (bf16[12288,128]{0,1:T(8,128)(2,1)S(1)}, bf16[12288,128]{0,1:T(8,128)(2,1)S(1)}, u32[]{:S(2)}, u32[]{:S(2)}) collective-permute-start(bf16[12288,128]{0,1:T(8,128)(2,1)S(1)} %pad_maximum_fusion.7), channel_id=1, source_target_pairs={{252,0},{0,4},{4,8},{8,12},{12,16},{16,20},{20,24},{24,28},{28,32}... | collective-permute-start | bytes 9437192 | tf_op jit(solution)/shard_map/ppermute | solution.py:17
Sparse Core Ops, SparseCore 0:
  179.6 45.7 all-reduce.2
  391.7 42.5 all-reduce.4
where the time goes:
time: 752 us; the launch traced here: 741 us
  waiting for transfers between devices  366 us (49%)
  blocking collectives  145 us (19%)
  other arithmetic  105 us (14%)
  local copies, waits for them, and re-layouts  60.8 us (8%)
  matrix products  28 us (4%)
  between operations  19.4 us (3%)
  starting transfers between devices  16.7 us (2%)
    all_to_all x1, blocking collectives, columns_layout(): lax.all_to_all(columns, 'blk', split_axis=0, concat_axis=1, tiled=True)  145 us
    ppermute x2, waiting for transfers between devices, from_behind(): return lax.ppermute(block, axis, route)  142 us
    all_to_all x1, waiting for transfers between devices, columns_layout(): lax.all_to_all(matrix, 'blk', split_axis=1, concat_axis=0, tiled=True)  135 us
    psum x2, waiting for transfers between devices, columns_layout(): gram_sums = lax.psum(gram_sums, 'row')  88.5 us
    another operation x12, other arithmetic, pair_rotation(): jnp.linalg.cholesky(identity + jnp.dot(cross.T, cross, precision=precise))  26.3 us
    another operation x12, other arithmetic, pair_rotation(): jnp.linalg.cholesky(identity + jnp.dot(cross, cross.T, precision=precise))  26.3 us
    psum x2, local copies, waits for them, and re-layouts, columns_layout(): gram_sums = lax.psum(gram_sums, 'row')  22.9 us
    another operation x8, other arithmetic, pair_rotation(): jax.scipy.linalg.solve_triangular(right_factor, identity, lower=True)  22.3 us
  transfers between devices with their start and end apart: 5, of which 5 were waited for; matrix products, arithmetic and copies ran while one was open for 0% of the time, Pallas kernels for 0%

commit v1 on v0

v1 whole, which is shorter than its diff:
```python
import functools
import jax
import jax.numpy as jnp
from jax import lax
from jax.experimental import pallas as pl
from jax.experimental.pallas import tpu as pltpu
from jax.sharding import PartitionSpec as P

BW = 64
STEPS = 2
XH, XL, NY, NZ = 2, 2, 4, 8
NX = XH * XL
CHUNKS = NX * NY
PER = NZ // 2
GROUPS = CHUNKS * PER
COUPLES = 2 * GROUPS
ROWS_LOC = 192
CROSS_ROWS = 16 * NZ
PAY = CROSS_ROWS + 16
WIDE = 256 * PER
MESH = pl.DeviceIdType.MESH
HIGH = lax.Precision.HIGHEST


def lanes(shape):
    return lax.broadcasted_iota(jnp.int32, shape, len(shape) - 1)


def group_gram(pair, base, xg, j, gscr, pay_ref, squares):
    gscr[...] = lax.dot_general(
        xg, xg, (((0,), (0,)), ((), ())), preferred_element_type=jnp.float32
    )
    eye = (
        lax.broadcasted_iota(jnp.int32, (128, 128), 0)
        == lax.broadcasted_iota(jnp.int32, (128, 128), 1)
    )
    sq = [
        jnp.sum(jnp.where(eye, gscr[128 * t : 128 * t + 128, 128 * t : 128 * t + 128], 0.0),
                axis=0, keepdims=True)
        for t in range(2)
    ]
    lane16 = lanes((16, 128)) < BW
    lane1 = lanes((1, 128)) < BW
    row16 = lax.broadcasted_iota(jnp.int32, (16, 128), 0)
    for c in range(2):
        a = pair[base + 2 * c]
        b = pair[base + 2 * c + 1]
        rows = gscr[pl.ds(pl.multiple_of(a * BW, BW), BW), :]
        tile = jnp.where(b >= 2, rows[:, 128:], rows[:, :128])
        turned = pltpu.roll(tile, BW, 1)
        odd = (b % 2) == 1
        low = jnp.where(odd, turned, tile)
        high = jnp.where(odd, tile, turned)
        n = 2 * j + c
        for h in range(2):
            pay_ref[h, 0, 16 * n : 16 * n + 16, :] = jnp.where(
                lane16, low[32 * h : 32 * h + 16], high[32 * h + 16 : 32 * h + 32]
            ).astype(jnp.bfloat16)
        sa = jnp.where(a >= 2, sq[1], sq[0])
        sa = jnp.where((a % 2) == 1, pltpu.roll(sa, BW, 1), sa)
        sb = jnp.where(b >= 2, sq[1], sq[0])
        sb = jnp.where(odd, sb, pltpu.roll(sb, BW, 1))
        squares = jnp.where(row16 == n, jnp.where(lane1, sa, sb), squares)
    return squares


def put_squares(squares, pay_ref):
    for h in range(2):
        pay_ref[h, 0, CROSS_ROWS:, :] = squares.astype(jnp.bfloat16)


def gram_body(pair, x_ref, pay_ref, gscr):
    i = pl.program_id(0)
    squares = jnp.zeros((16, 128), jnp.float32)
    for j in range(PER):
        squares = group_gram(
            pair, (i * PER + j) * 4, x_ref[:, 256 * j : 256 * j + 256], j, gscr, pay_ref, squares
        )
    put_squares(squares, pay_ref)


def gram_call(pair, x):
    return pl.pallas_call(
        gram_body,
        out_shape=jax.ShapeDtypeStruct((2, CHUNKS, PAY, 128), jnp.bfloat16),
        grid_spec=pltpu.PrefetchScalarGridSpec(
            num_scalar_prefetch=1,
            grid=(CHUNKS,),
            in_specs=[pl.BlockSpec((ROWS_LOC, WIDE), lambda i, p: (0, i))],
            out_specs=pl.BlockSpec((2, 1, PAY, 128), lambda i, p: (0, i, 0, 0)),
            scratch_shapes=[pltpu.VMEM((256, 256), jnp.float32)],
        ),
    )(pair, x)


def rotate_group(pair, base, xg, left, right, wscr):
    lane = lanes((BW, 128)) < BW
    zero = jnp.zeros((BW, 128), jnp.bfloat16)
    for c in range(2):
        a = pair[base + 2 * c]
        b = pair[base + 2 * c + 1]
        top = jnp.where(lane, left[c], right[c])
        bot = pltpu.roll(jnp.where(lane, right[c], left[c]), BW, 1)
        for s in range(4):
            wscr[BW * s : BW * s + BW, 128 * c : 128 * c + 128] = jnp.where(
                a == s, top, jnp.where(b == s, bot, zero)
            )
    return jnp.dot(xg, wscr[...], preferred_element_type=jnp.float32).astype(jnp.bfloat16)


def apply_body(with_gram, pair, pair_next, x_ref, rot_ref, xlast_ref, rotlast_ref, *rest):
    if with_gram:
        out_ref, pay_ref, wscr, carry, gscr = rest
    else:
        out_ref, wscr, carry = rest
    i = pl.program_id(0)

    @pl.when(i == 0)
    def _():
        carry[...] = rotate_group(
            pair, (GROUPS - 1) * 4, xlast_ref[...],
            [rotlast_ref[0, c] for c in range(2)], [rotlast_ref[1, c] for c in range(2)], wscr,
        )

    keep = (lanes((ROWS_LOC, 256)) % 128) < BW
    squares = jnp.zeros((16, 128), jnp.float32)
    for j in range(PER):
        g = i * PER + j
        y = rotate_group(
            pair, g * 4, x_ref[:, 256 * j : 256 * j + 256],
            [rot_ref[0, 2 * j + c] for c in range(2)],
            [rot_ref[1, 2 * j + c] for c in range(2)], wscr,
        )
        out = jnp.where(keep, y, carry[...])
        carry[...] = y
        out_ref[:, 256 * j : 256 * j + 256] = out
        if with_gram:
            squares = group_gram(pair_next, g * 4, out, j, gscr, pay_ref, squares)
    if with_gram:
        put_squares(squares, pay_ref)


def apply_call(pair, pair_next, x, rot, with_gram):
    out_shape = [jax.ShapeDtypeStruct(x.shape, jnp.bfloat16)]
    out_specs = [pl.BlockSpec((ROWS_LOC, WIDE), lambda i, p, q: (0, i))]
    scratch = [pltpu.VMEM((256, 256), jnp.bfloat16), pltpu.VMEM((ROWS_LOC, 256), jnp.bfloat16)]
    if with_gram:
        out_shape.append(jax.ShapeDtypeStruct((2, CHUNKS, PAY, 128), jnp.bfloat16))
        out_specs.append(pl.BlockSpec((2, 1, PAY, 128), lambda i, p, q: (0, i, 0, 0)))
        scratch.append(pltpu.VMEM((256, 256), jnp.float32))
    return pl.pallas_call(
        functools.partial(apply_body, with_gram),
        out_shape=out_shape,
        grid_spec=pltpu.PrefetchScalarGridSpec(
            num_scalar_prefetch=2,
            grid=(CHUNKS,),
            in_specs=[
                pl.BlockSpec((ROWS_LOC, WIDE), lambda i, p, q: (0, i)),
                pl.BlockSpec((2, NZ, BW, 128), lambda i, p, q: (0, i, 0, 0)),
                pl.BlockSpec((ROWS_LOC, 256), lambda i, p, q: (0, GROUPS - 1)),
                pl.BlockSpec((2, 2, BW, 128), lambda i, p, q: (0, GROUPS - 1, 0, 0)),
            ],
            out_specs=out_specs,
            scratch_shapes=scratch,
        ),
    )(pair, pair_next, x, rot, x, rot)


def half_rotation(own0, own1, squares, core):
    raw = jnp.concatenate(
        [own0[:, :BW], own0[:, BW:], own1[:, :BW], own1[:, BW:]], axis=0
    )
    scale = 1.0 / jnp.sqrt(squares + 1e-06)
    row = lax.broadcasted_iota(jnp.int32, (BW, BW), 0)
    col = lax.broadcasted_iota(jnp.int32, (BW, BW), 1)
    eye = row == col
    left_scale = jnp.sum(jnp.where(eye, scale[:, :BW], 0.0), axis=1, keepdims=True)
    cross = 0.5 * raw * left_scale * scale[:, BW:]
    crossed = cross.T
    is_left = core == 0
    y = jnp.where(is_left, cross, crossed)
    yt = jnp.where(is_left, crossed, cross)
    unit = jnp.where(eye, 1.0, 0.0)
    full = unit + jnp.dot(y, yt, precision=HIGH, preferred_element_type=jnp.float32)
    m = jnp.concatenate([full, unit], axis=1)
    below = lax.broadcasted_iota(jnp.int32, (BW, 1), 0)
    pivots = None
    for k in range(BW):
        pivot_row = m[k : k + 1, :]
        inverse = 1.0 / m[k : k + 1, k : k + 1]
        factor = jnp.where(below > k, m[:, k : k + 1], 0.0) * inverse
        m = m - factor * pivot_row
    diag = jnp.sum(jnp.where(eye, m[:, :BW], 0.0), axis=1, keepdims=True)
    lower = m[:, BW:] * lax.rsqrt(diag)
    upper = lower.T
    other = jnp.dot(yt, upper, precision=HIGH, preferred_element_type=jnp.float32)
    first = upper
    second = jnp.where(is_left, -other, other)
    return jnp.concatenate([first, second], axis=1).astype(jnp.bfloat16)


def comm_body(pay, out, got0, sent1, got1, sent2, got2, *sems):
    (ss0, rs0, ss1, rs1, ss2, rs2, ss4, rs4, ss5, rs5, ss6, rs6, ss7, rs7) = sems
    row, blk = lax.axis_index("row"), lax.axis_index("blk")
    core = lax.rem(row, 2)
    z = lax.rem(blk, NZ)
    x = (row // 2) * XL + lax.rem(blk // NZ, XL)
    y = blk // (NZ * XL)
    sibling = 1 - core

    def device(x, y, z, core):
        return {"row": (x // XL) * 2 + core, "blk": (y * XL + lax.rem(x, XL)) * NZ + z}

    def ahead(v, d, n):
        return lax.rem(v + d, n)

    def behind(v, d, n):
        return lax.rem(v + (n - d), n)

    own = x * NY + y
    own_pos = own * NZ + z
    pending = []

    def send(src, dst, send_sem, recv_sem, target):
        copy = pltpu.make_async_remote_copy(
            src_ref=src, dst_ref=dst, send_sem=send_sem, recv_sem=recv_sem,
            device_id=target, device_id_type=MESH,
        )
        copy.start()
        pending.append(copy)

    def arrived(dst, send_sem, recv_sem):
        pltpu.make_async_remote_copy(
            src_ref=dst, dst_ref=dst, send_sem=send_sem, recv_sem=recv_sem,
            device_id=device(x, y, z, sibling), device_id_type=MESH,
        ).wait_recv()

    def plane(d):
        there = ahead(own, d, CHUNKS)
        return there // NY, lax.rem(there, NY)

    barrier = pltpu.get_barrier_semaphore()
    greeted = [device(*plane(d), z, core) for d in range(1, CHUNKS)]
    greeted += [
        device(x, y, ahead(z, dz, NZ), ahead(core, dc, 2))
        for dz in range(NZ) for dc in range(2) if dz or dc
    ]
    for peer in greeted:
        pl.semaphore_signal(barrier, inc=1, device_id=peer, device_id_type=MESH)
    pl.semaphore_wait(barrier, len(greeted))

    order = list(range(1, CHUNKS)) + [0]
    for d in order:
        send(pay.at[sibling, ahead(own, d, CHUNKS)], got0.at[d], ss0.at[d], rs0.at[d],
             device(x, y, z, sibling))
    for d in order:
        arrived(got0.at[d], ss0.at[d], rs0.at[d])
        both = pay[core, ahead(own, d, CHUNKS)].astype(jnp.float32) + got0[d].astype(jnp.float32)
        if d == 0:
            total = both
        else:
            sent1[d] = both.astype(jnp.bfloat16)
            send(sent1.at[d], got1.at[d], ss1.at[d], rs1.at[d], device(*plane(d), z, core))
    for d in range(1, CHUNKS):
        arrived(got1.at[d], ss1.at[d], rs1.at[d])
        total = total + got1[d].astype(jnp.float32)
    for there in range(NZ):
        sent2[there, :16] = total[16 * there : 16 * there + 16]
        sent2[there, 16:] = total[CROSS_ROWS : CROSS_ROWS + 8]
    for dz in range(NZ):
        for dc in range(2):
            if dz or dc:
                there = ahead(z, dz, NZ)
                send(sent2.at[there], got2.at[core, dz], ss2.at[dc, dz], rs2.at[dc, dz],
                     device(x, y, there, ahead(core, dc, 2)))
    got2[core, 0] = sent2[z]
    for dz in range(NZ):
        for dc in range(2):
            if dz or dc:
                arrived(got2.at[ahead(core, dc, 2), dz], ss2.at[dc, dz], rs2.at[dc, dz])
    halves = [sum([got2[h, dz] for dz in range(1, NZ)], got2[h, 0]) for h in range(2)]
    pick = lax.broadcasted_iota(jnp.int32, (8, 128), 0) == z
    squares = jnp.sum(jnp.where(pick, halves[0][16:], 0.0), axis=0, keepdims=True)
    out[core, own_pos] = half_rotation(halves[0][:16], halves[1][:16], squares, core)

    for dz in range(1, NZ):
        send(out.at[core, own_pos], out.at[core, own_pos], ss4.at[dz], rs4.at[dz],
             device(x, y, ahead(z, dz, NZ), core))
    for dz in range(1, NZ):
        arrived(out.at[core, own * NZ + behind(z, dz, NZ)], ss4.at[dz], rs4.at[dz])

    def block(which, e, f):
        bx = behind(x, which * e + (1 - which) * f, NX)
        by = behind(y, (1 - which) * e + which * f, NY)
        return out.at[which, pl.ds((bx * NY + by) * NZ, NZ)]

    def along(e, f):
        return device(
            ahead(x, core * e + (1 - core) * f, NX), ahead(y, (1 - core) * e + core * f, NY),
            z, core,
        )

    def forward(e, f):
        send(block(core, e, f), block(core, e, f), ss7.at[e, f], rs7.at[e, f],
             device(x, y, z, sibling))

    for e in range(1, NX):
        send(block(core, 0, 0), block(core, 0, 0), ss5.at[e], rs5.at[e], along(e, 0))
    for e in range(NX):
        if e:
            arrived(block(core, e, 0), ss5.at[e], rs5.at[e])
        for f in range(1, NX):
            send(block(core, e, 0), block(core, e, 0), ss6.at[e, f], rs6.at[e, f], along(0, f))
        forward(e, 0)
    for e in range(NX):
        for f in range(1, NX):
            arrived(block(core, e, f), ss6.at[e, f], rs6.at[e, f])
            forward(e, f)
    for e in range(NX):
        for f in range(NX):
            arrived(block(sibling, e, f), ss7.at[e, f], rs7.at[e, f])
    for copy in pending:
        copy.wait_send()


def exchange(pay):
    dma = pltpu.SemaphoreType.DMA
    shapes = [(CHUNKS,), (CHUNKS,), (2, NZ), (NZ,), (NX,), (NX, NX), (NX, NX)]
    return pl.pallas_call(
        comm_body,
        out_shape=jax.ShapeDtypeStruct((2, COUPLES, BW, 128), jnp.bfloat16),
        in_specs=[pl.BlockSpec(memory_space=pltpu.VMEM)],
        out_specs=pl.BlockSpec(memory_space=pltpu.VMEM),
        scratch_shapes=[
            pltpu.VMEM((CHUNKS, PAY, 128), jnp.bfloat16),
            pltpu.VMEM((CHUNKS, PAY, 128), jnp.bfloat16),
            pltpu.VMEM((CHUNKS, PAY, 128), jnp.bfloat16),
            pltpu.VMEM((NZ, 24, 128), jnp.float32),
            pltpu.VMEM((2, NZ, 24, 128), jnp.float32),
        ]
        + [dma(shape) for shape in shapes for _ in range(2)],
        compiler_params=pltpu.CompilerParams(
            collective_id=0, has_side_effects=True, vmem_limit_bytes=32 * 2**20
        ),
    )(pay)


def local(matrix, pairing):
    flat = pairing.reshape(STEPS, GROUPS * 4)
    pay = gram_call(flat[0], matrix)
    rot = exchange(pay)
    current, pay = apply_call(flat[0], flat[1], matrix, rot, True)
    rot = exchange(pay)
    return apply_call(flat[1], flat[1], current, rot, False)[0]


def solution(mesh):
    placed = (P(("row", "blk"), None), P())
    return jax.shard_map(
        local, mesh=mesh, in_specs=placed, out_specs=P(("row", "blk"), None), check_vma=False
    )
```

time: 752 us -> 185 us (0.25); the launches traced: 741 us -> 184 us
  waiting for transfers between devices: 366 us -> 0 us
  Pallas kernels: 0 us -> 175 us
  blocking collectives: 145 us -> 0 us
  other arithmetic: 105 us -> 0 us
  local copies, waits for them, and re-layouts: 60.8 us -> 8.78 us
  matrix products: 28 us -> 0 us
  between operations: 19.4 us -> 0.04 us
  starting transfers between devices: 16.7 us -> 0 us
    pallas_call x0 -> x5, Pallas kernels: none -> 175 us  [the longest x2 127 us: exchange(): pl.pallas_call(comm_body, out_shape=jax.ShapeDtypeStruct((2, COUPLES, BW,...]
    all_to_all x1 -> x0, blocking collectives: 145 us -> none  [columns_layout(): lax.all_to_all(columns, 'blk', split_axis=0, concat_axis=1, tiled=True)]
    ppermute x2 -> x0, waiting for transfers between devices: 142 us -> none  [from_behind(): return lax.ppermute(block, axis, route)]
    all_to_all x1 -> x0, waiting for transfers between devices: 135 us -> none  [columns_layout(): lax.all_to_all(matrix, 'blk', split_axis=1, concat_axis=0, tiled=True)]
    another operation x42 -> x0, other arithmetic: 98.6 us -> none  [the longest x12 26.3 us: pair_rotation(): jnp.linalg.cholesky(identity + jnp.dot(cross.T, cross, precision=precise))]
    psum x2 -> x0, waiting for transfers between devices: 88.5 us -> none  [columns_layout(): gram_sums = lax.psum(gram_sums, 'row')]
    dot_general x24 -> x0, matrix products: 26.6 us -> none  [the longest x4 12.6 us: columns_layout(): jnp.dot(couples[which], pair_rotation(crosses[which], squares[which]), pr...]
    psum x2 -> x0, local copies, waits for them, and re-layouts: 22.9 us -> none  [columns_layout(): gram_sums = lax.psum(gram_sums, 'row')]
  transfers between devices with their start and end apart: 5 -> 0, of which waited for: 5 -> 0; matrix products, arithmetic and copies ran while one was open for 0% -> 0% of each run, Pallas kernels for 0% -> 0%
where the time goes in v1:
time: 185 us; the launch traced here: 184 us
  Pallas kernels  175 us (95%)
  local copies, waits for them, and re-layouts  8.78 us (5%)
    pallas_call x2, Pallas kernels, exchange(): pl.pallas_call(comm_body, out_shape=jax.ShapeDtypeStruct((2, COUPLES, BW,...  127 us
    pallas_call x2, Pallas kernels, apply_call(): pl.pallas_call(functools.partial(apply_body, with_gram), out_shape=out_sh...  34.4 us
    pallas_call x1, Pallas kernels, gram_call(): pl.pallas_call(gram_body, out_shape=jax.ShapeDtypeStruct((2, CHUNKS, PAY,...  14.1 us
    unnamed x8, local copies, waits for them, and re-layouts  6.57 us

profile of v1, /device:TPU:1, one launch (start us, length us, event | category | flops | bytes accessed | tf_op | source)
XLA Modules:
  0.0 184.1 jit_solution(4606580756251879122)
XLA Ops:
  0.0 0.7 fusion
  0.7 0.1 copy.4
  0.8 0.7 squeeze.10.pair
  1.5 0.1 copy.3
  1.6 0.6 squeeze.4.pair_next.pair
  2.2 14.1 %shard_map.28.pay = bf16[2,16,144,128]{3,2,1,0:T(8,128)(2,1)} custom-call(s32[256]{0:T(256)} %squeeze.10.pair, bf16[192,16384]{1,0:T(8,128)(2,1)} %xlast_ref.1), custom_call_target="tpu_custom_call" | custom-call | tf_op jit(solution)/shard_map/pallas_call | solution.py:83
  16.3 0.0 copy-start.2
  16.3 1.3 copy-done.2
  17.6 65.8 %shard_map.29.rot_ref.rotlast_ref = bf16[2,128,64,128]{3,2,1,0:T(8,128)(2,1)S(1)} custom-call(bf16[2,16,144,128]{3,2,1,0:T(8,128)(2,1)S(1)} %copy-done.2), custom_call_target="tpu_custom_call" | custom-call | tf_op jit(solution)/shard_map/pallas_call | solution.py:329
  83.4 0.0 copy-start
  83.4 2.0 %copy-done = bf16[2,128,64,128]{3,2,1,0:T(8,128)(2,1)} copy-done((bf16[2,128,64,128]{3,2,1,0:T(8,128)(2,1)}, bf16[2,128,64,128]{3,2,1,0:T(8,128)(2,1)S(1)}, u32[]{:S(2)}) %copy-start) | copy-done | bytes 4194328
  85.4 18.6 %shard_map.30 = (bf16[192,16384]{1,0:T(8,128)(2,1)}, bf16[2,16,144,128]{3,2,1,0:T(8,128)(2,1)}) custom-call(s32[256]{0:T(256)} %squeeze.10.pair, s32[256]{0:T(256)} %squeeze.4.pair_next.pair, bf16[192,16384]{1,0:T(8,128)(2,1)} %xlast_ref.1, bf16[2,128,64,128]{3,2,1,0:T(8,128)(2,1)} %copy-done, bf16[192,16384]{1,0:T(8,128)(2,1)} %xlast_ref.1, ...), custom_call_target="tpu_custom_call" | custom-call | tf_op jit(solution)/shard_map/pallas_call | solution.py:151
  104.0 0.0 copy-start.3
  104.0 1.3 copy-done.3
  105.3 61.0 %shard_map.31.rot_ref.rotlast_ref = bf16[2,128,64,128]{3,2,1,0:T(8,128)(2,1)S(1)} custom-call(bf16[2,16,144,128]{3,2,1,0:T(8,128)(2,1)S(1)} %copy-done.3), custom_call_target="tpu_custom_call" | custom-call | tf_op jit(solution)/shard_map/pallas_call | solution.py:329
  166.3 0.0 copy-start.1
  166.3 2.0 %copy-done.1 = bf16[2,128,64,128]{3,2,1,0:T(8,128)(2,1)} copy-done((bf16[2,128,64,128]{3,2,1,0:T(8,128)(2,1)}, bf16[2,128,64,128]{3,2,1,0:T(8,128)(2,1)S(1)}, u32[]{:S(2)}) %copy-start.1) | copy-done | bytes 4194328
  168.3 15.8 %shard_map.32 = bf16[192,16384]{1,0:T(8,128)(2,1)} custom-call(s32[256]{0:T(256)} %squeeze.4.pair_next.pair, s32[256]{0:T(256)} %squeeze.4.pair_next.pair, bf16[192,16384]{1,0:T(8,128)(2,1)} %get-tuple-element.7.x_ref.xlast_ref, bf16[2,128,64,128]{3,2,1,0:T(8,128)(2,1)} %copy-done.1, bf16[192,16384]{1,0:T(8,128)(2,1)} %get-tuple-element.7.x_ref.xlast_ref, ...), custom_call_target="tpu_custom_call" | custom-call | tf_op jit(solution)/shard_map/pallas_call | solution.py:151
Async XLA Ops:
  16.3 1.3 copy-start.2
  83.4 2.0 %copy-start = (bf16[2,128,64,128]{3,2,1,0:T(8,128)(2,1)}, bf16[2,128,64,128]{3,2,1,0:T(8,128)(2,1)S(1)}, u32[]{:S(2)}) copy-start(bf16[2,128,64,128]{3,2,1,0:T(8,128)(2,1)S(1)} %shard_map.29.rot_ref.rotlast_ref) | copy-start | bytes 12582916
  104.0 1.3 copy-start.3
  166.3 2.0 %copy-start.1 = (bf16[2,128,64,128]{3,2,1,0:T(8,128)(2,1)}, bf16[2,128,64,128]{3,2,1,0:T(8,128)(2,1)S(1)}, u32[]{:S(2)}) copy-start(bf16[2,128,64,128]{3,2,1,0:T(8,128)(2,1)S(1)} %shard_map.31.rot_ref.rotlast_ref) | copy-start | bytes 12582916

commit v2 on v0

v2 whole, which is shorter than its diff:
```python
import jax
import jax.numpy as jnp
from jax import lax
from jax.experimental import pallas as pl
from jax.experimental.pallas import tpu as pltpu
from jax.sharding import PartitionSpec as P

BW = 64
STEPS = 2
XH, XL, NY, NZ = 2, 2, 4, 8
NX = XH * XL
CHUNKS = NX * NY
PER = NZ // 2
GROUPS = CHUNKS * PER
ROWS_LOC = 192
CROSS_ROWS = 32 * PER
PAY = CROSS_ROWS + 16
WIDE = 256 * PER
LAG = 2
HIGH = lax.Precision.HIGHEST
MESH = pl.DeviceIdType.MESH
ORDER = [(0, 0), (1, 0), (3, 0), (0, 1), (0, 3), (1, 1), (3, 3), (1, 3), (3, 1),
         (2, 0), (0, 2), (2, 1), (1, 2), (2, 3), (3, 2), (2, 2)]


def lanes(shape):
    return lax.broadcasted_iota(jnp.int32, shape, len(shape) - 1)


def gram_of(xg):
    return lax.dot_general(
        xg, xg, (((0,), (0,)), ((), ())), preferred_element_type=jnp.float32
    )


def group_payload(slots, j, gscr):
    row = lax.broadcasted_iota(jnp.int32, (BW, 128), 0)
    lane = lanes((BW, 128))
    sq = []
    for t in range(2):
        tile = slice(128 * t, 128 * t + 128)
        first = jnp.where(lane == row, gscr[j, 128 * t : 128 * t + BW, tile], 0.0)
        second = jnp.where(lane == row + BW, gscr[j, 128 * t + BW : 128 * t + 128, tile], 0.0)
        sq.append(jnp.sum(first + second, axis=0, keepdims=True))
    turned_sq = [pltpu.roll(v, BW, 1) for v in sq]
    lane32 = lanes((32, 128)) < BW
    lane1 = lanes((1, 128)) < BW
    cross, squares = [], []
    for c in range(2):
        a, b = slots[2 * c], slots[2 * c + 1]
        high_b = jnp.broadcast_to(b >= 2, (BW, 128))
        tile = None
        for s in range(4):
            rows = slice(BW * s, BW * s + BW)
            part = jnp.where(high_b, gscr[j, rows, 128:], gscr[j, rows, :128])
            tile = part if tile is None else jnp.where(
                jnp.broadcast_to(a == s, (BW, 128)), part, tile
            )
        turned = pltpu.roll(tile, BW, 1)
        odd_b = (b == 1) | (b == 3)
        odd = jnp.broadcast_to(odd_b, (32, 128))
        low = jnp.where(odd, turned[:32], tile[:32])
        high = jnp.where(odd, tile[32:], turned[32:])
        cross.append(jnp.where(lane32, low, high).astype(jnp.bfloat16))
        sa = jnp.where(a == 0, sq[0], jnp.where(
            a == 1, turned_sq[0], jnp.where(a == 2, sq[1], turned_sq[1])))
        sb = jnp.where(b == 0, turned_sq[0], jnp.where(
            b == 1, sq[0], jnp.where(b == 2, turned_sq[1], sq[1])))
        squares.append(jnp.where(lane1, sa, sb))
    return cross, squares


def rotate_group(slots, xg, left, right):
    lane = lanes((BW, 128)) < BW
    zero = jnp.zeros((BW, 128), jnp.bfloat16)
    tiles = []
    for c in range(2):
        a, b = [jnp.broadcast_to(slots[2 * c + k], (BW, 128)) for k in range(2)]
        top = jnp.where(lane, left[c], right[c])
        bot = pltpu.roll(jnp.where(lane, right[c], left[c]), BW, 1)
        tiles.append(jnp.concatenate(
            [jnp.where(a == s, top, jnp.where(b == s, bot, zero)) for s in range(4)], axis=0
        ))
    return jnp.dot(
        xg, jnp.concatenate(tiles, axis=1), preferred_element_type=jnp.float32
    ).astype(jnp.bfloat16)


def half_rotations(packed, squares):
    raw = jnp.concatenate([packed[:, :BW], packed[:, BW:]], axis=0)
    scale = 1.0 / jnp.sqrt(squares + 1e-06)
    row = lax.broadcasted_iota(jnp.int32, (BW, BW), 0)
    col = lax.broadcasted_iota(jnp.int32, (BW, BW), 1)
    eye = row == col
    left_scale = jnp.sum(jnp.where(eye, scale[:, :BW], 0.0), axis=1, keepdims=True)
    cross = 0.5 * raw * left_scale * scale[:, BW:]
    crossed = cross.T
    unit = jnp.where(eye, 1.0, 0.0)
    below = lax.broadcasted_iota(jnp.int32, (BW, 1), 0)
    pairs = [(cross, crossed), (crossed, cross)]
    work = [
        jnp.concatenate(
            [unit + jnp.dot(u, v, precision=HIGH, preferred_element_type=jnp.float32), unit],
            axis=1,
        )
        for u, v in pairs
    ]
    for k in range(BW):
        for side in range(2):
            m = work[side]
            inverse = 1.0 / m[k : k + 1, k : k + 1]
            factor = jnp.where(below > k, m[:, k : k + 1], 0.0)
            work[side] = m - factor * (m[k : k + 1, :] * inverse)
    halves = []
    for side in range(2):
        m = work[side]
        diag = jnp.sum(jnp.where(eye, m[:, :BW], 0.0), axis=1, keepdims=True)
        upper = (m[:, BW:] * lax.rsqrt(diag)).T
        other = jnp.dot(
            pairs[side][1], upper, precision=HIGH, preferred_element_type=jnp.float32
        )
        halves.append(jnp.concatenate([upper, other if side else -other], axis=1))
    return [half.astype(jnp.bfloat16) for half in halves]


def body(pair, matrix, out, cur, gscr, pay, got0, sent1, got1, sent2, got2, rot, *sems):
    (ins, ss0, rs0, ss1, rs1, ss2, rs2, ss4, rs4, ss5, rs5, ss6, rs6, ss7, rs7, outs, edges) = sems
    row, blk = lax.axis_index("row"), lax.axis_index("blk")
    core = lax.rem(row, 2)
    z = lax.rem(blk, NZ)
    x = (row // 2) * XL + lax.rem(blk // NZ, XL)
    y = blk // (NZ * XL)
    sibling = 1 - core
    own = x * NY + y
    mine = z // 2
    owner = lax.rem(z, 2) == core

    def device(x, y, z, core):
        return {"row": (x // XL) * 2 + core, "blk": (y * XL + lax.rem(x, XL)) * NZ + z}

    beside = device(x, y, z, sibling)

    def ahead(v, d, n):
        return lax.rem(v + d, n)

    def behind(v, d, n):
        return lax.rem(v + (n - d), n)

    def plane(d):
        there = ahead(own, d, CHUNKS)
        return device(there // NY, lax.rem(there, NY), z, core)

    def copy(src, dst, send_sem, recv_sem, target):
        return pltpu.make_async_remote_copy(
            src_ref=src, dst_ref=dst, send_sem=send_sem, recv_sem=recv_sem,
            device_id=target, device_id_type=MESH,
        )

    def columns(chunk, first=0, count=WIDE):
        return pl.ds(pl.multiple_of(chunk * WIDE + first, 256), count)

    def load(s):
        at = columns(ahead(own, s + 1, CHUNKS))
        return pltpu.make_async_copy(matrix.at[:, at], cur.at[0, :, at], ins.at[s])

    @pl.loop(0, CHUNKS)
    def _(s):
        load(s).start()

    barrier = pltpu.get_barrier_semaphore()
    greeted = [plane(d) for d in range(1, CHUNKS)] + [beside]
    greeted += [device(x, y, ahead(z, dz, NZ), core) for dz in range(1, NZ)]
    for peer in greeted:
        pl.semaphore_signal(barrier, inc=1, device_id=peer, device_id_type=MESH)
    pl.semaphore_wait(barrier, len(greeted))

    def turn(t):
        src, dst = t % 2, (t + 1) % 2

        def slots_of(chunk):
            numbers = pair[pl.ds(t * CHUNKS + chunk, 1), :]
            return [
                [jnp.broadcast_to(numbers[:, n : n + 1], (1, 128)) for n in range(4 * j, 4 * j + 4)]
                for j in range(PER)
            ]

        def core_copy(s):
            return copy(pay.at[t, s, sibling], got0.at[t, s], ss0.at[t, s], rs0.at[t, s], beside)

        def plane_copy(s):
            return copy(sent1.at[t, s], got1.at[t, s], ss1.at[t, s], rs1.at[t, s], plane(s + 1))

        def summed(s):
            core_copy(s).wait_recv()
            return pay[t, s, core].astype(jnp.float32) + got0[t, s].astype(jnp.float32)

        def pass_on(s):
            sent1[t, s] = summed(s).astype(jnp.bfloat16)
            plane_copy(s).start()

        @pl.loop(0, CHUNKS)
        def _(s):
            chunk = ahead(own, s + 1, CHUNKS)
            if t == 0:
                load(s).wait()
            for j in range(PER):
                at = pl.ds(pl.multiple_of(chunk * WIDE + 256 * j, 256), 256)
                gscr[j] = gram_of(cur[src, :, at])
            slots = slots_of(chunk)
            row16 = lax.broadcasted_iota(jnp.int32, (16, 128), 0)
            squares = [jnp.zeros((16, 128), jnp.float32)] * 2
            for j in range(PER):
                cross, sq = group_payload(slots[j], j, gscr)
                for c in range(2):
                    pay[t, s, c, 32 * j : 32 * j + 32] = cross[c]
                    squares[c] = jnp.where(row16 == j, sq[c], squares[c])
            for c in range(2):
                pay[t, s, c, CROSS_ROWS:] = squares[c].astype(jnp.bfloat16)
            core_copy(s).start()

            @pl.when(s >= LAG)
            def _():
                pass_on(s - LAG)

        @pl.loop(CHUNKS - LAG, CHUNKS - 1)
        def _(s):
            pass_on(s)

        total = summed(CHUNKS - 1)
        for s in range(CHUNKS - 1):
            plane_copy(s).wait_recv()
            total = total + got1[t, s].astype(jnp.float32)

        for j in range(PER):
            sent2[t, j, :32] = total[32 * j : 32 * j + 32]
            sent2[t, j, 32:] = total[CROSS_ROWS : CROSS_ROWS + 8]

        def sum_copy(dz):
            there = ahead(z, dz, NZ)
            return copy(sent2.at[t, there // 2], got2.at[t, dz], ss2.at[t, dz], rs2.at[t, dz],
                        device(x, y, there, core))

        def gather_copy(dz, at):
            piece = rot.at[t, core, own, at]
            return copy(piece, piece, ss4.at[t, dz], rs4.at[t, dz],
                        device(x, y, ahead(z, dz, NZ), core))

        @pl.when(owner)
        def _():
            for dz in range(2, NZ, 2):
                sum_copy(dz).start()
            got = sent2[t, mine]
            for dz in range(1, NZ):
                sum_copy(dz).wait_recv()
                got = got + got2[t, dz]
            pick = lax.broadcasted_iota(jnp.int32, (8, 128), 0) == mine
            squares = jnp.sum(jnp.where(pick, got[32:], 0.0), axis=0, keepdims=True)
            halves = half_rotations(got[:32], squares)
            for side in range(2):
                rot[t, core, own, mine, side] = halves[side]
            for dz in range(1, NZ):
                gather_copy(dz, mine).start()
            for dz in range(2, NZ, 2):
                gather_copy(dz, behind(z, dz, NZ) // 2).wait_recv()
            for dz in range(2, NZ, 2):
                sum_copy(dz).wait_send()
            for dz in range(1, NZ):
                gather_copy(dz, mine).wait_send()

        @pl.when(jnp.logical_not(owner))
        def _():
            for dz in range(1, NZ, 2):
                sum_copy(dz).start()
            for dz in range(1, NZ, 2):
                gather_copy(dz, behind(z, dz, NZ) // 2).wait_recv()
            for dz in range(1, NZ, 2):
                sum_copy(dz).wait_send()

        def where(e, f):
            bx = behind(x, core * e + (1 - core) * f, NX)
            by = behind(y, (1 - core) * e + core * f, NY)
            return bx * NY + by

        def block(which, e, f, part=None):
            piece = rot.at[t, which, where(e, f)]
            return piece if part is None else piece.at[pl.ds(part * (PER // 2), PER // 2)]

        def along(e, f):
            return device(
                ahead(x, core * e + (1 - core) * f, NX),
                ahead(y, (1 - core) * e + core * f, NY), z, core,
            )

        def first_copy(e):
            return copy(block(core, 0, 0), block(core, 0, 0), ss5.at[t, e], rs5.at[t, e],
                        along(e, 0))

        def second_copy(e, f):
            piece = block(core, e, 0)
            return copy(piece, piece, ss6.at[t, e, f], rs6.at[t, e, f], along(0, f))

        def second_wait(e, f):
            piece = block(core, e, f)
            copy(piece, piece, ss6.at[t, e, f], rs6.at[t, e, f], beside).wait_recv()

        def relay_copy(e, f):
            piece = block(core, e, f, f // 2)
            k = f - f // 2 * 3
            return copy(piece, piece, ss6.at[t, e, 2 * k], rs6.at[t, e, 2 * k], along(0, f))

        def relay_wait(e, f):
            piece = block(core, e, 2, f // 2)
            k = f - f // 2 * 3
            copy(piece, piece, ss6.at[t, e, 2 * k], rs6.at[t, e, 2 * k], beside).wait_recv()

        def to_core(e, f):
            piece = block(core, e, f)
            return copy(piece, piece, ss7.at[t, e, f], rs7.at[t, e, f], beside)

        def core_wait(e, f):
            piece = block(sibling, e, f)
            copy(piece, piece, ss7.at[t, f, e], rs7.at[t, f, e], beside).wait_recv()

        for e in range(1, NX):
            first_copy(e).start()
        for e in (0, 1, 3, 2):
            if e:
                piece = block(core, e, 0)
                copy(piece, piece, ss5.at[t, e], rs5.at[t, e], beside).wait_recv()
            second_copy(e, 1).start()
            second_copy(e, 3).start()
            to_core(e, 0).start()

        def relay(e):
            for f in (1, 3):
                second_wait(e, f)
                relay_copy(e, f).start()
                to_core(e, f).start()

        def last(e):
            relay_wait(e, 1)
            relay_wait(e, 3)
            to_core(e, 2).start()

        events = {0: [(relay, 0)], 1: [(relay, 1)], 3: [(relay, 3)], 5: [(relay, 2)],
                  8: [(last, 0), (last, 1)], 9: [(last, 3), (last, 2)]}

        def out_copy(k):
            e, f = nth(k)
            at = columns(where(e, f), 256, WIDE - 256)
            return pltpu.make_async_copy(cur.at[dst, :, at], out.at[:, at], outs.at[k])

        def edge_copy(i):
            at = columns(i, 0, 256)
            return pltpu.make_async_copy(cur.at[dst, :, at], out.at[:, at], edges.at[i])

        def nth(k):
            e = sum(jnp.where(k == n, v[0], 0) for n, v in enumerate(ORDER) if v[0])
            f = sum(jnp.where(k == n, v[1], 0) for n, v in enumerate(ORDER) if v[1])
            return e, f

        keep = lax.rem(lanes((ROWS_LOC, 256)), 128) < BW

        @pl.loop(0, CHUNKS)
        def _(k):
            for n, steps in events.items():
                @pl.when(k == n)
                def _():
                    for step, e in steps:
                        step(e)

            e, f = nth(k)
            core_wait(e, f)
            chunk = where(e, f)
            slots = slots_of(chunk)
            before = None
            for j in range(PER):
                at = pl.ds(pl.multiple_of(chunk * WIDE + 256 * j, 256), 256)
                now = rotate_group(
                    slots[j], cur[src, :, at],
                    [rot[t, c, chunk, j, 0] for c in range(2)],
                    [rot[t, c, chunk, j, 1] for c in range(2)],
                )
                odd = cur[dst, :, at] if before is None else before
                cur[dst, :, at] = jnp.where(keep, now, odd)
                before = now
            at = columns(ahead(chunk, 1, CHUNKS), 0, 256)
            cur[dst, :, at] = jnp.where(keep, cur[dst, :, at], before)
            if t == STEPS - 1:
                out_copy(k).start()

        if t == STEPS - 1:
            @pl.loop(0, CHUNKS)
            def _(i):
                edge_copy(i).start()

            @pl.loop(0, CHUNKS)
            def _(i):
                out_copy(i).wait()
                edge_copy(i).wait()

        @pl.loop(0, CHUNKS)
        def _(s):
            core_copy(s).wait_send()

        @pl.loop(0, CHUNKS - 1)
        def _(s):
            plane_copy(s).wait_send()

        for e in range(1, NX):
            first_copy(e).wait_send()

        @pl.loop(0, NX)
        def _(e):
            for f in (1, 3):
                second_copy(e, f).wait_send()
                relay_copy(e, f).wait_send()
            for f in range(NX):
                to_core(e, f).wait_send()

    for t in range(STEPS):
        turn(t)


def local(matrix, pairing):
    dma = pltpu.SemaphoreType.DMA
    shapes = [(CHUNKS,), (CHUNKS,), (NZ,), (NZ,), (NX,), (NX, 5), (NX, NX)]
    vmem = pltpu.VMEM
    return pl.pallas_call(
        body,
        out_shape=jax.ShapeDtypeStruct(matrix.shape, matrix.dtype),
        in_specs=[pl.BlockSpec(memory_space=pltpu.VMEM), pl.BlockSpec(memory_space=pl.ANY)],
        out_specs=pl.BlockSpec(memory_space=pl.ANY),
        scratch_shapes=[
            vmem((2, ROWS_LOC, 256 * GROUPS), jnp.bfloat16),
            vmem((PER, 256, 256), jnp.float32),
            vmem((STEPS, CHUNKS, 2, PAY, 128), jnp.bfloat16),
            vmem((STEPS, CHUNKS, PAY, 128), jnp.bfloat16),
            vmem((STEPS, CHUNKS - 1, PAY, 128), jnp.bfloat16),
            vmem((STEPS, CHUNKS - 1, PAY, 128), jnp.bfloat16),
            vmem((STEPS, PER, 40, 128), jnp.float32),
            vmem((STEPS, NZ, 40, 128), jnp.float32),
            vmem((STEPS, 2, CHUNKS, PER, 2, BW, 128), jnp.bfloat16),
        ]
        + [dma((CHUNKS,))]
        + [dma((STEPS,) + shape) for shape in shapes for _ in range(2)]
        + [dma((CHUNKS,))] * 2,
        compiler_params=pltpu.CompilerParams(
            collective_id=0, has_side_effects=True, vmem_limit_bytes=48 * 2**20
        ),
    )(pairing.reshape(STEPS * CHUNKS, 4 * PER), matrix)


def solution(mesh):
    placed = (P(("row", "blk"), None), P())
    return jax.shard_map(
        local, mesh=mesh, in_specs=placed, out_specs=P(("row", "blk"), None), check_vma=False
    )
```

time: 752 us -> 143 us (0.19); the launches traced: 741 us -> 143 us
  waiting for transfers between devices: 366 us -> 0 us
  blocking collectives: 145 us -> 0 us
  Pallas kernels: 0 us -> 136 us
  other arithmetic: 105 us -> 0 us
  local copies, waits for them, and re-layouts: 60.8 us -> 6.95 us
  matrix products: 28 us -> 0 us
  between operations: 19.4 us -> 0.02 us
  starting transfers between devices: 16.7 us -> 0 us
    all_to_all x1 -> x0, blocking collectives: 145 us -> none  [columns_layout(): lax.all_to_all(columns, 'blk', split_axis=0, concat_axis=1, tiled=True)]
    ppermute x2 -> x0, waiting for transfers between devices: 142 us -> none  [from_behind(): return lax.ppermute(block, axis, route)]
    pallas_call x0 -> x1, Pallas kernels: none -> 136 us  [local(): pl.pallas_call(body, out_shape=jax.ShapeDtypeStruct(matrix.shape, matrix....]
    all_to_all x1 -> x0, waiting for transfers between devices: 135 us -> none  [columns_layout(): lax.all_to_all(matrix, 'blk', split_axis=1, concat_axis=0, tiled=True)]
    another operation x42 -> x0, other arithmetic: 98.6 us -> none  [the longest x12 26.3 us: pair_rotation(): jnp.linalg.cholesky(identity + jnp.dot(cross.T, cross, precision=precise))]
    psum x2 -> x0, waiting for transfers between devices: 88.5 us -> none  [columns_layout(): gram_sums = lax.psum(gram_sums, 'row')]
    dot_general x24 -> x0, matrix products: 26.6 us -> none  [the longest x4 12.6 us: columns_layout(): jnp.dot(couples[which], pair_rotation(crosses[which], squares[which]), pr...]
    psum x2 -> x0, local copies, waits for them, and re-layouts: 22.9 us -> none  [columns_layout(): gram_sums = lax.psum(gram_sums, 'row')]
  transfers between devices with their start and end apart: 5 -> 0, of which waited for: 5 -> 0; matrix products, arithmetic and copies ran while one was open for 0% -> 0% of each run, Pallas kernels for 0% -> 0%
where the time goes in v2:
time: 143 us
  Pallas kernels  136 us (95%)
  local copies, waits for them, and re-layouts  6.95 us (5%)
    pallas_call x1, Pallas kernels, local(): pl.pallas_call(body, out_shape=jax.ShapeDtypeStruct(matrix.shape, matrix....  136 us
    unnamed x2, local copies, waits for them, and re-layouts  6.88 us

profile of v2, /device:TPU:1, one launch (start us, length us, event | category | flops | bytes accessed | tf_op | source)
XLA Modules:
  0.0 142.8 jit_solution(12182291015723447433)
XLA Ops:
  0.0 0.8 copy.4
  0.8 0.1 reshape.3.pair
  0.9 135.8 %shard_map.28 = bf16[192,16384]{1,0:T(8,128)(2,1)} custom-call(s32[32,16]{1,0:T(8,128)S(1)} %reshape.3.pair, bf16[192,16384]{1,0:T(8,128)(2,1)} %matrix.1), custom_call_target="tpu_custom_call" | custom-call | tf_op jit(solution)/shard_map/pallas_call | solution.py:429
  136.7 6.1 %copy.6 = bf16[192,16384]{1,0:T(8,128)(2,1)} copy(bf16[192,16384]{1,0:T(8,128)(2,1)} %shard_map.28) | data formatting | bytes 12582912

commit v3 on v2

--- a/solution.py
+++ b/solution.py
@@ -19,8 +19,8 @@
 LAG = 2
 HIGH = lax.Precision.HIGHEST
 MESH = pl.DeviceIdType.MESH
-ORDER = [(0, 0), (1, 0), (3, 0), (0, 1), (0, 3), (1, 1), (3, 3), (1, 3), (3, 1),
-         (2, 0), (0, 2), (2, 1), (1, 2), (2, 3), (3, 2), (2, 2)]
+ORDER = [(0, 0), (0, 1), (0, 3), (1, 0), (3, 0), (1, 1), (1, 3), (3, 1), (3, 3),
+         (0, 2), (2, 0), (1, 2), (2, 1), (3, 2), (2, 3), (2, 2)]
 
 
 def lanes(shape):
@@ -96,7 +96,7 @@
     cross = 0.5 * raw * left_scale * scale[:, BW:]
     crossed = cross.T
     unit = jnp.where(eye, 1.0, 0.0)
-    below = lax.broadcasted_iota(jnp.int32, (BW, 1), 0)
+    number = lax.broadcasted_iota(jnp.int32, (BW, 1), 0)
     pairs = [(cross, crossed), (crossed, cross)]
     work = [
         jnp.concatenate(
@@ -105,12 +105,29 @@
         )
         for u, v in pairs
     ]
-    for k in range(BW):
+    for k in range(0, BW - 2, 2):
         for side in range(2):
             m = work[side]
-            inverse = 1.0 / m[k : k + 1, k : k + 1]
-            factor = jnp.where(below > k, m[:, k : k + 1], 0.0)
-            work[side] = m - factor * (m[k : k + 1, :] * inverse)
+            p, q, r = [
+                jnp.broadcast_to(m[i : i + 1, j : j + 1], (1, 128))
+                for i, j in ((k, k), (k, k + 1), (k + 1, k + 1))
+            ]
+            inverse = 1.0 / (p * r - q * q)
+            over, under = m[k : k + 1, :], m[k + 1 : k + 2, :]
+            one = (r * over - q * under) * inverse
+            two = (p * under - q * over) * inverse
+            below = number > k + 1
+            work[side] = m - (
+                jnp.where(below, m[:, k : k + 1], 0.0) * one
+                + jnp.where(below, m[:, k + 1 : k + 2], 0.0) * two
+            )
+    for side in range(2):
+        m = work[side]
+        pivot = jnp.sum(jnp.where(eye, m[:, :BW], 0.0), axis=1, keepdims=True)
+        beside = jnp.sum(jnp.where(row == col + 1, m[:, :BW], 0.0), axis=1, keepdims=True)
+        above = pltpu.roll(jnp.broadcast_to(pivot, (BW, 128)), 1, 0)
+        odd = jnp.where(lax.rem(number, 2) == 1, beside, 0.0)
+        work[side] = m - odd / above * pltpu.roll(m, 1, 0)
     halves = []
     for side in range(2):
         m = work[side]
@@ -124,7 +141,7 @@
 
 
 def body(pair, matrix, out, cur, gscr, pay, got0, sent1, got1, sent2, got2, rot, *sems):
-    (ins, ss0, rs0, ss1, rs1, ss2, rs2, ss4, rs4, ss5, rs5, ss6, rs6, ss7, rs7, outs, edges) = sems
+    (ins, ss0, rs0, ss1, rs1, ss2, rs2, ss4, rs4, ss5, rs5, ss6, rs6, ss7, rs7) = sems
     row, blk = lax.axis_index("row"), lax.axis_index("blk")
     core = lax.rem(row, 2)
     z = lax.rem(blk, NZ)
@@ -172,10 +189,9 @@
     greeted += [device(x, y, ahead(z, dz, NZ), core) for dz in range(1, NZ)]
     for peer in greeted:
         pl.semaphore_signal(barrier, inc=1, device_id=peer, device_id_type=MESH)
-    pl.semaphore_wait(barrier, len(greeted))
 
     def turn(t):
-        src, dst = t % 2, (t + 1) % 2
+        src, dst = cur.at[t], cur.at[1] if t == 0 else out
 
         def slots_of(chunk):
             numbers = pair[pl.ds(t * CHUNKS + chunk, 1), :]
@@ -205,7 +221,7 @@
                 load(s).wait()
             for j in range(PER):
                 at = pl.ds(pl.multiple_of(chunk * WIDE + 256 * j, 256), 256)
-                gscr[j] = gram_of(cur[src, :, at])
+                gscr[j] = gram_of(src[:, at])
             slots = slots_of(chunk)
             row16 = lax.broadcasted_iota(jnp.int32, (16, 128), 0)
             squares = [jnp.zeros((16, 128), jnp.float32)] * 2
@@ -216,6 +232,11 @@
                     squares[c] = jnp.where(row16 == j, sq[c], squares[c])
             for c in range(2):
                 pay[t, s, c, CROSS_ROWS:] = squares[c].astype(jnp.bfloat16)
+            if t == 0:
+                @pl.when(s == 0)
+                def _():
+                    pl.semaphore_wait(barrier, len(greeted))
+
             core_copy(s).start()
 
             @pl.when(s >= LAG)
@@ -342,17 +363,8 @@
             relay_wait(e, 3)
             to_core(e, 2).start()
 
-        events = {0: [(relay, 0)], 1: [(relay, 1)], 3: [(relay, 3)], 5: [(relay, 2)],
-                  8: [(last, 0), (last, 1)], 9: [(last, 3), (last, 2)]}
-
-        def out_copy(k):
-            e, f = nth(k)
-            at = columns(where(e, f), 256, WIDE - 256)
-            return pltpu.make_async_copy(cur.at[dst, :, at], out.at[:, at], outs.at[k])
-
-        def edge_copy(i):
-            at = columns(i, 0, 256)
-            return pltpu.make_async_copy(cur.at[dst, :, at], out.at[:, at], edges.at[i])
+        events = {1: [(relay, 0)], 3: [(relay, 1)], 5: [(relay, 3)], 6: [(relay, 2)],
+                  9: [(last, 0)], 11: [(last, 1)], 13: [(last, 3)], 15: [(last, 2)]}
 
         def nth(k):
             e = sum(jnp.where(k == n, v[0], 0) for n, v in enumerate(ORDER) if v[0])
@@ -377,27 +389,15 @@
             for j in range(PER):
                 at = pl.ds(pl.multiple_of(chunk * WIDE + 256 * j, 256), 256)
                 now = rotate_group(
-                    slots[j], cur[src, :, at],
+                    slots[j], src[:, at],
                     [rot[t, c, chunk, j, 0] for c in range(2)],
                     [rot[t, c, chunk, j, 1] for c in range(2)],
                 )
-                odd = cur[dst, :, at] if before is None else before
-                cur[dst, :, at] = jnp.where(keep, now, odd)
+                odd = dst[:, at] if before is None else before
+                dst[:, at] = jnp.where(keep, now, odd)
                 before = now
             at = columns(ahead(chunk, 1, CHUNKS), 0, 256)
-            cur[dst, :, at] = jnp.where(keep, cur[dst, :, at], before)
-            if t == STEPS - 1:
-                out_copy(k).start()
-
-        if t == STEPS - 1:
-            @pl.loop(0, CHUNKS)
-            def _(i):
-                edge_copy(i).start()
-
-            @pl.loop(0, CHUNKS)
-            def _(i):
-                out_copy(i).wait()
-                edge_copy(i).wait()
+            dst[:, at] = jnp.where(keep, dst[:, at], before)
 
         @pl.loop(0, CHUNKS)
         def _(s):
@@ -428,9 +428,9 @@
     vmem = pltpu.VMEM
     return pl.pallas_call(
         body,
-        out_shape=jax.ShapeDtypeStruct(matrix.shape, matrix.dtype),
+        out_shape=pltpu.VMEM(matrix.shape, matrix.dtype),
         in_specs=[pl.BlockSpec(memory_space=pltpu.VMEM), pl.BlockSpec(memory_space=pl.ANY)],
-        out_specs=pl.BlockSpec(memory_space=pl.ANY),
+        out_specs=pl.BlockSpec(memory_space=pltpu.VMEM),
         scratch_shapes=[
             vmem((2, ROWS_LOC, 256 * GROUPS), jnp.bfloat16),
             vmem((PER, 256, 256), jnp.float32),
@@ -443,8 +443,7 @@
             vmem((STEPS, 2, CHUNKS, PER, 2, BW, 128), jnp.bfloat16),
         ]
         + [dma((CHUNKS,))]
-        + [dma((STEPS,) + shape) for shape in shapes for _ in range(2)]
-        + [dma((CHUNKS,))] * 2,
+        + [dma((STEPS,) + shape) for shape in shapes for _ in range(2)],
         compiler_params=pltpu.CompilerParams(
             collective_id=0, has_side_effects=True, vmem_limit_bytes=48 * 2**20
         ),

time: 143 us -> 128 us (0.90)
  Pallas kernels: 136 us -> 124 us
  local copies, waits for them, and re-layouts: 6.95 us -> 4.18 us
    pallas_call x1, Pallas kernels: 136 us -> 124 us  [local(): pl.pallas_call(body, out_shape=pltpu.VMEM(matrix.shape, matrix.dtype), in...]
    unnamed x2, local copies, waits for them, and re-layouts: 6.88 us -> 3.49 us
where the time goes in v3:
time: 128 us
  Pallas kernels  124 us (97%)
  local copies, waits for them, and re-layouts  4.18 us (3%)
    pallas_call x1, Pallas kernels, local(): pl.pallas_call(body, out_shape=pltpu.VMEM(matrix.shape, matrix.dtype), in...  124 us
    unnamed x2, local copies, waits for them, and re-layouts  3.49 us

profile of v3, /device:TPU:1, one launch (start us, length us, event | category | flops | bytes accessed | tf_op | source)
XLA Modules:
  0.0 128.1 jit_solution(1450858469443702454)
XLA Ops:
  0.0 0.8 copy.4
  0.8 0.7 reshape.3.pair
  1.5 123.9 %shard_map.28 = bf16[192,16384]{1,0:T(8,128)(2,1)S(1)} custom-call(s32[32,16]{1,0:T(8,128)} %reshape.3.pair, bf16[192,16384]{1,0:T(8,128)(2,1)} %matrix.1), custom_call_target="tpu_custom_call" | custom-call | tf_op jit(solution)/shard_map/pallas_call | solution.py:429
  125.4 2.7 %copy.6 = bf16[192,16384]{1,0:T(8,128)(2,1)} copy(bf16[192,16384]{1,0:T(8,128)(2,1)S(1)} %shard_map.28) | data formatting | bytes 12582912

commit v4 on v3

--- a/solution.py
+++ b/solution.py
@@ -16,7 +16,6 @@
 CROSS_ROWS = 32 * PER
 PAY = CROSS_ROWS + 16
 WIDE = 256 * PER
-LAG = 2
 HIGH = lax.Precision.HIGHEST
 MESH = pl.DeviceIdType.MESH
 ORDER = [(0, 0), (0, 1), (0, 3), (1, 0), (3, 0), (1, 1), (1, 3), (3, 1), (3, 3),
@@ -194,11 +193,14 @@
         src, dst = cur.at[t], cur.at[1] if t == 0 else out
 
         def slots_of(chunk):
-            numbers = pair[pl.ds(t * CHUNKS + chunk, 1), :]
-            return [
-                [jnp.broadcast_to(numbers[:, n : n + 1], (1, 128)) for n in range(4 * j, 4 * j + 4)]
-                for j in range(PER)
-            ]
+            table = pair[t].astype(jnp.float32)
+            lane = lanes(table.shape)
+            slots = []
+            for j in range(PER):
+                picked = jnp.where(lane == chunk * PER + j, table, 0.0)
+                numbers = jnp.sum(picked, axis=1, keepdims=True)
+                slots.append([jnp.broadcast_to(numbers[n : n + 1], (1, 128)) for n in range(4)])
+            return slots
 
         def core_copy(s):
             return copy(pay.at[t, s, sibling], got0.at[t, s], ss0.at[t, s], rs0.at[t, s], beside)
@@ -214,39 +216,43 @@
             sent1[t, s] = summed(s).astype(jnp.bfloat16)
             plane_copy(s).start()
 
-        @pl.loop(0, CHUNKS)
-        def _(s):
+        def gram_chunk(s, u):
             chunk = ahead(own, s + 1, CHUNKS)
-            if t == 0:
-                load(s).wait()
             for j in range(PER):
                 at = pl.ds(pl.multiple_of(chunk * WIDE + 256 * j, 256), 256)
-                gscr[j] = gram_of(src[:, at])
+                gscr[u, j] = gram_of(src[:, at])
             slots = slots_of(chunk)
             row16 = lax.broadcasted_iota(jnp.int32, (16, 128), 0)
             squares = [jnp.zeros((16, 128), jnp.float32)] * 2
             for j in range(PER):
-                cross, sq = group_payload(slots[j], j, gscr)
+                cross, sq = group_payload(slots[j], j, gscr.at[u])
                 for c in range(2):
                     pay[t, s, c, 32 * j : 32 * j + 32] = cross[c]
                     squares[c] = jnp.where(row16 == j, sq[c], squares[c])
             for c in range(2):
                 pay[t, s, c, CROSS_ROWS:] = squares[c].astype(jnp.bfloat16)
+
+        @pl.loop(0, CHUNKS // 2)
+        def _(k):
             if t == 0:
-                @pl.when(s == 0)
+                for u in range(2):
+                    load(2 * k + u).wait()
+            for u in range(2):
+                gram_chunk(2 * k + u, u)
+            if t == 0:
+                @pl.when(k == 0)
                 def _():
                     pl.semaphore_wait(barrier, len(greeted))
 
-            core_copy(s).start()
-
-            @pl.when(s >= LAG)
+            for u in range(2):
+                core_copy(2 * k + u).start()
+
+            @pl.when(k > 0)
             def _():
-                pass_on(s - LAG)
-
-        @pl.loop(CHUNKS - LAG, CHUNKS - 1)
-        def _(s):
-            pass_on(s)
-
+                for u in range(2):
+                    pass_on(2 * k - 2 + u)
+
+        pass_on(CHUNKS - 2)
         total = summed(CHUNKS - 1)
         for s in range(CHUNKS - 1):
             plane_copy(s).wait_recv()
@@ -363,8 +369,8 @@
             relay_wait(e, 3)
             to_core(e, 2).start()
 
-        events = {1: [(relay, 0)], 3: [(relay, 1)], 5: [(relay, 3)], 6: [(relay, 2)],
-                  9: [(last, 0)], 11: [(last, 1)], 13: [(last, 3)], 15: [(last, 2)]}
+        events = {0: [(relay, 0)], 1: [(relay, 1)], 2: [(relay, 3)], 3: [(relay, 2)],
+                  4: [(last, 0)], 5: [(last, 1)], 6: [(last, 3)], 7: [(last, 2)]}
 
         def nth(k):
             e = sum(jnp.where(k == n, v[0], 0) for n, v in enumerate(ORDER) if v[0])
@@ -373,17 +379,7 @@
 
         keep = lax.rem(lanes((ROWS_LOC, 256)), 128) < BW
 
-        @pl.loop(0, CHUNKS)
-        def _(k):
-            for n, steps in events.items():
-                @pl.when(k == n)
-                def _():
-                    for step, e in steps:
-                        step(e)
-
-            e, f = nth(k)
-            core_wait(e, f)
-            chunk = where(e, f)
+        def rotate_chunk(chunk):
             slots = slots_of(chunk)
             before = None
             for j in range(PER):
@@ -399,6 +395,20 @@
             at = columns(ahead(chunk, 1, CHUNKS), 0, 256)
             dst[:, at] = jnp.where(keep, dst[:, at], before)
 
+        @pl.loop(0, CHUNKS // 2)
+        def _(k):
+            for n, steps in events.items():
+                @pl.when(k == n)
+                def _():
+                    for step, e in steps:
+                        step(e)
+
+            both = [nth(2 * k + u) for u in range(2)]
+            for e, f in both:
+                core_wait(e, f)
+            for e, f in both:
+                rotate_chunk(where(e, f))
+
         @pl.loop(0, CHUNKS)
         def _(s):
             core_copy(s).wait_send()
@@ -433,7 +443,7 @@
         out_specs=pl.BlockSpec(memory_space=pltpu.VMEM),
         scratch_shapes=[
             vmem((2, ROWS_LOC, 256 * GROUPS), jnp.bfloat16),
-            vmem((PER, 256, 256), jnp.float32),
+            vmem((2, PER, 256, 256), jnp.float32),
             vmem((STEPS, CHUNKS, 2, PAY, 128), jnp.bfloat16),
             vmem((STEPS, CHUNKS, PAY, 128), jnp.bfloat16),
             vmem((STEPS, CHUNKS - 1, PAY, 128), jnp.bfloat16),
@@ -447,7 +457,7 @@
         compiler_params=pltpu.CompilerParams(
             collective_id=0, has_side_effects=True, vmem_limit_bytes=48 * 2**20
         ),
-    )(pairing.reshape(STEPS * CHUNKS, 4 * PER), matrix)
+    )(jnp.transpose(pairing, (0, 2, 1)), matrix)
 
 
 def solution(mesh):

time: 128 us -> 121 us (0.945)
  Pallas kernels: 124 us -> 118 us
  local copies, waits for them, and re-layouts: 4.18 us -> 2.71 us
    pallas_call x1, Pallas kernels: 124 us -> 118 us  [local(): pl.pallas_call(body, out_shape=pltpu.VMEM(matrix.shape, matrix.dtype), in...]
    unnamed x2 -> x1, local copies, waits for them, and re-layouts: 3.49 us -> 2.71 us
where the time goes in v4:
time: 121 us
  Pallas kernels  118 us (98%)
  local copies, waits for them, and re-layouts  2.71 us (2%)
    pallas_call x1, Pallas kernels, local(): pl.pallas_call(body, out_shape=pltpu.VMEM(matrix.shape, matrix.dtype), in...  118 us
    unnamed x1, local copies, waits for them, and re-layouts  2.71 us

profile of v4, /device:TPU:1, one launch (start us, length us, event | category | flops | bytes accessed | tf_op | source)
XLA Modules:
  0.0 121.1 jit_solution(12908207035880550397)
XLA Ops:
  0.0 118.4 %shard_map.28 = bf16[192,16384]{1,0:T(8,128)(2,1)S(1)} custom-call(s32[2,4,64]{2,1,0:T(4,128)} %bitcast.1, bf16[192,16384]{1,0:T(8,128)(2,1)} %matrix.1), custom_call_target="tpu_custom_call" | custom-call | tf_op jit(solution)/shard_map/pallas_call | solution.py:439
  118.4 2.7 %copy.4 = bf16[192,16384]{1,0:T(8,128)(2,1)} copy(bf16[192,16384]{1,0:T(8,128)(2,1)S(1)} %shard_map.28) | data formatting | bytes 12582912

commit v5 on v4

--- a/solution.py
+++ b/solution.py
@@ -272,6 +272,33 @@
             return copy(piece, piece, ss4.at[t, dz], rs4.at[t, dz],
                         device(x, y, ahead(z, dz, NZ), core))
 
+        def where(e, f):
+            bx = behind(x, core * e + (1 - core) * f, NX)
+            by = behind(y, (1 - core) * e + core * f, NY)
+            return bx * NY + by
+
+        def block(which, e, f, part=None):
+            piece = rot.at[t, which, where(e, f)]
+            return piece if part is None else piece.at[pl.ds(part * (PER // 2), PER // 2)]
+
+        def along(e, f):
+            return device(
+                ahead(x, core * e + (1 - core) * f, NX),
+                ahead(y, (1 - core) * e + core * f, NY), z, core,
+            )
+
+        def first_copy(e, j):
+            piece = rot.at[t, core, own, j]
+            return copy(piece, piece, ss5.at[t, e, j], rs5.at[t, e, j], along(e, 0))
+
+        def first_wait(e, j):
+            piece = rot.at[t, core, where(e, 0), j]
+            copy(piece, piece, ss5.at[t, e, j], rs5.at[t, e, j], beside).wait_recv()
+
+        def spread(j):
+            for e in range(1, NX):
+                first_copy(e, j).start()
+
         @pl.when(owner)
         def _():
             for dz in range(2, NZ, 2):
@@ -287,8 +314,10 @@
                 rot[t, core, own, mine, side] = halves[side]
             for dz in range(1, NZ):
                 gather_copy(dz, mine).start()
-            for dz in range(2, NZ, 2):
+            spread(mine)
+            for dz in (2, 6, 4):
                 gather_copy(dz, behind(z, dz, NZ) // 2).wait_recv()
+                spread(behind(z, dz, NZ) // 2)
             for dz in range(2, NZ, 2):
                 sum_copy(dz).wait_send()
             for dz in range(1, NZ):
@@ -298,29 +327,11 @@
         def _():
             for dz in range(1, NZ, 2):
                 sum_copy(dz).start()
-            for dz in range(1, NZ, 2):
+            for dz in (1, 7, 3, 5):
                 gather_copy(dz, behind(z, dz, NZ) // 2).wait_recv()
+                spread(behind(z, dz, NZ) // 2)
             for dz in range(1, NZ, 2):
                 sum_copy(dz).wait_send()
-
-        def where(e, f):
-            bx = behind(x, core * e + (1 - core) * f, NX)
-            by = behind(y, (1 - core) * e + core * f, NY)
-            return bx * NY + by
-
-        def block(which, e, f, part=None):
-            piece = rot.at[t, which, where(e, f)]
-            return piece if part is None else piece.at[pl.ds(part * (PER // 2), PER // 2)]
-
-        def along(e, f):
-            return device(
-                ahead(x, core * e + (1 - core) * f, NX),
-                ahead(y, (1 - core) * e + core * f, NY), z, core,
-            )
-
-        def first_copy(e):
-            return copy(block(core, 0, 0), block(core, 0, 0), ss5.at[t, e], rs5.at[t, e],
-                        along(e, 0))
 
         def second_copy(e, f):
             piece = block(core, e, 0)
@@ -348,12 +359,10 @@
             piece = block(sibling, e, f)
             copy(piece, piece, ss7.at[t, f, e], rs7.at[t, f, e], beside).wait_recv()
 
-        for e in range(1, NX):
-            first_copy(e).start()
         for e in (0, 1, 3, 2):
             if e:
-                piece = block(core, e, 0)
-                copy(piece, piece, ss5.at[t, e], rs5.at[t, e], beside).wait_recv()
+                for j in range(PER):
+                    first_wait(e, j)
             second_copy(e, 1).start()
             second_copy(e, 3).start()
             to_core(e, 0).start()
@@ -418,7 +427,8 @@
             plane_copy(s).wait_send()
 
         for e in range(1, NX):
-            first_copy(e).wait_send()
+            for j in range(PER):
+                first_copy(e, j).wait_send()
 
         @pl.loop(0, NX)
         def _(e):
@@ -434,7 +444,7 @@
 
 def local(matrix, pairing):
     dma = pltpu.SemaphoreType.DMA
-    shapes = [(CHUNKS,), (CHUNKS,), (NZ,), (NZ,), (NX,), (NX, 5), (NX, NX)]
+    shapes = [(CHUNKS,), (CHUNKS,), (NZ,), (NZ,), (NX, PER), (NX, 5), (NX, NX)]
     vmem = pltpu.VMEM
     return pl.pallas_call(
         body,

time: 121 us -> 117 us (0.967)
  Pallas kernels: 118 us -> 114 us
    pallas_call x1, Pallas kernels: 118 us -> 114 us  [local(): pl.pallas_call(body, out_shape=pltpu.VMEM(matrix.shape, matrix.dtype), in...]
where the time goes in v5:
time: 117 us
  Pallas kernels  114 us (97%)
  local copies, waits for them, and re-layouts  2.71 us (2%)
    pallas_call x1, Pallas kernels, local(): pl.pallas_call(body, out_shape=pltpu.VMEM(matrix.shape, matrix.dtype), in...  114 us
    unnamed x1, local copies, waits for them, and re-layouts  2.71 us

profile of v5, /device:TPU:1, one launch (start us, length us, event | category | flops | bytes accessed | tf_op | source)
XLA Modules:
  0.0 116.9 jit_solution(3269753823790051444)
XLA Ops:
  0.0 114.1 %shard_map.28 = bf16[192,16384]{1,0:T(8,128)(2,1)S(1)} custom-call(s32[2,4,64]{2,1,0:T(4,128)} %bitcast.1, bf16[192,16384]{1,0:T(8,128)(2,1)} %matrix.1), custom_call_target="tpu_custom_call" | custom-call | tf_op jit(solution)/shard_map/pallas_call | solution.py:449
  114.1 2.7 %copy.4 = bf16[192,16384]{1,0:T(8,128)(2,1)} copy(bf16[192,16384]{1,0:T(8,128)(2,1)S(1)} %shard_map.28) | data formatting | bytes 12582912
